TPU v7x, 32 devices: a whole 2x2x4 slice. The times are simulated.
32 devices in a mesh: fsdp: 2 (over y), blk: 4 (over x, core), ulysses: 4 (over z).
Axes of the slice: x: 2, y: 2, z: 4, core: 2. Of those that a mesh axis runs over, the one named last changes fastest.
Arguments:
- tokens: bfloat16 [8192, 768], P(('fsdp', 'blk', 'ulysses')), may hold values from -6 to 6
- positions: int32 [8192], P(('fsdp', 'blk', 'ulysses')), may hold values from 0 to 4095, as said below
- cotangent: bfloat16 [8192, 768], P(('fsdp', 'blk', 'ulysses')), may hold values from -6 to 6
- ln1_gain: bfloat16 [768], P('fsdp'), may hold values from 0.099609375 to 1.8984375
- ln1_bias: bfloat16 [768], P('fsdp'), may hold values from -3 to 3
- ln2_gain: bfloat16 [768], P('fsdp'), may hold values from 0.099609375 to 1.8984375
- ln2_bias: bfloat16 [768], P('fsdp'), may hold values from -3 to 3
- qkv_weight: bfloat16 [768, 2304], P('fsdp'), may hold values from -0.21875 to 0.21875
- qkv_bias: bfloat16 [2304], P('fsdp'), may hold values from -2 to 2
- out_weight: bfloat16 [768, 768], P('fsdp'), may hold values from -3 to 3
- out_bias: bfloat16 [768], P('fsdp'), may hold values from -2 to 2
- up_weight: bfloat16 [768, 3072], P('fsdp'), may hold values from -0.21875 to 0.21875
- up_bias: bfloat16 [3072], P('fsdp'), may hold values from -2 to 2
- down_weight: bfloat16 [3072, 768], P('fsdp'), may hold values from -0.109375 to 0.109375
- down_bias: bfloat16 [768], P('fsdp'), may hold values from -2 to 2
Outputs:
- output: bfloat16 [8192, 768], P(('fsdp', 'blk', 'ulysses'))
- input_grad: bfloat16 [8192, 768], P(('fsdp', 'blk', 'ulysses'))
- ln1_gain_grad: float32 [768], P('fsdp')
- ln1_bias_grad: float32 [768], P('fsdp')
- ln2_gain_grad: float32 [768], P('fsdp')
- ln2_bias_grad: float32 [768], P('fsdp')
- qkv_weight_grad: float32 [768, 2304], P('fsdp')
- qkv_bias_grad: float32 [2304], P('fsdp')
- out_weight_grad: float32 [768, 768], P('fsdp')
- out_bias_grad: float32 [768], P('fsdp')
- up_weight_grad: float32 [768, 3072], P('fsdp')
- up_bias_grad: float32 [3072], P('fsdp')
- down_weight_grad: float32 [3072, 768], P('fsdp')
- down_bias_grad: float32 [768], P('fsdp')
Inputs may be any that keep to these rules, and one draw needn't show every extreme that they name: Each sequence of 4096 tokens holds every position from 0 once; positions run in blocks of 128 consecutive ascending values, and the order of the blocks within a sequence is drawn.
All inputs are finite; a program needn't handle non-finite values.
Results may differ from a plain program's by a relative error of at most 0.018.
Values may be sent and summed in bfloat16 or wider, within the bound.
No kernel may reach another device: no remote copies, remote signals or barrier semaphores. Data moves between devices by JAX's collectives and lax.ppermute only.
A program may use at most 128 MiB of HBM per device.

v0:
```python
import jax
import jax.numpy as jnp
from jax import lax
from jax.sharding import PartitionSpec as P

HEAD = 64
ROT = 16


BIG_NEG = -1e30


def shortened(shard):
    return jax.tree.map(lambda a: a.astype(jnp.bfloat16) if a.dtype == jnp.float32 else a, shard)


def layer_norm(values, gain, shift):
    center = jnp.mean(values, -1, keepdims=True)
    offset = values - center
    spread = jnp.mean(offset * offset, -1, keepdims=True)
    return offset * lax.rsqrt(spread + 1e-05) * gain + shift


def gelu_exact(values):
    return jax.nn.gelu(values, approximate=False)


def rotate(values, places, turn):
    count = values.shape[0]
    cols = values.shape[1]
    heads = values.reshape(count, cols // HEAD, HEAD)
    halfway = ROT // 2
    freqs = 10000.0 ** (-(jnp.arange(halfway, dtype=jnp.float32) * 2.0) / ROT)
    angles = places.astype(jnp.float32)[:, None] * freqs[None, :]
    cosine = jnp.cos(angles)[:, None, :]
    sine = jnp.sin(angles)[:, None, :] * turn
    first = heads[..., :halfway]
    second = heads[..., halfway:ROT]
    turned = jnp.concatenate(
        [first * cosine - second * sine, second * cosine + first * sine, heads[..., ROT:]], -1
    )
    return turned.reshape(count, cols)


def score_grads(
    query_block,
    grad_block,
    query_places,
    block_total,
    block_delta,
    key_block,
    value_block,
    key_places,
):
    scores = jnp.einsum(
        "qhd,khd->hqk", query_block, key_block, preferred_element_type=jnp.float32
    ) * HEAD ** (-0.5)
    allowed = (key_places[None, :] <= query_places[:, None])[None]
    scores = jnp.where(allowed, scores, BIG_NEG)
    probs = jnp.where(allowed, jnp.exp(scores - block_total[..., None]), 0.0)
    d_probs = jnp.einsum(
        "qhd,khd->hqk", grad_block, value_block, preferred_element_type=jnp.float32
    )
    d_scores = (probs * (d_probs - block_delta[..., None])).astype(jnp.bfloat16)
    return (probs, d_scores)


def on_device(
    tokens,
    positions,
    cotangent,
    ln1_gain,
    ln1_bias,
    ln2_gain,
    ln2_bias,
    qkv_weight,
    qkv_bias,
    out_weight,
    out_bias,
    up_weight,
    up_bias,
    down_weight,
    down_bias,
):
    f32 = jnp.float32
    bf16 = jnp.bfloat16
    gathered = (
        lax.all_gather(ln1_gain, "fsdp", axis=0, tiled=True),
        lax.all_gather(ln1_bias, "fsdp", axis=0, tiled=True),
        lax.all_gather(ln2_gain, "fsdp", axis=0, tiled=True),
        lax.all_gather(ln2_bias, "fsdp", axis=0, tiled=True),
        lax.all_gather(qkv_weight, "fsdp", axis=0, tiled=True),
        lax.all_gather(qkv_bias, "fsdp", axis=0, tiled=True),
        lax.all_gather(out_weight, "fsdp", axis=0, tiled=True),
        lax.all_gather(out_bias, "fsdp", axis=0, tiled=True),
        lax.all_gather(up_weight, "fsdp", axis=0, tiled=True),
        lax.all_gather(up_bias, "fsdp", axis=0, tiled=True),
        lax.all_gather(down_weight, "fsdp", axis=0, tiled=True),
        lax.all_gather(down_bias, "fsdp", axis=0, tiled=True),
    )
    ln1_g, ln1_b, ln2_g, ln2_b, w_qkv, b_qkv, w_out, b_out, w_up, b_up, w_down, b_down = gathered
    tok_count = tokens.shape[0]
    model_width = tokens.shape[1]
    groups = lax.axis_size("ulysses")
    head_rows = tok_count * groups
    local_cols = model_width // groups
    local_heads = local_cols // HEAD
    scale = HEAD ** (-0.5)
    order_all = lax.all_gather(positions, ("blk", "ulysses"), axis=0, tiled=True)
    seq_len = order_all.shape[0]
    head_places = lax.dynamic_slice_in_dim(order_all, lax.axis_index("blk") * head_rows, head_rows)
    x_float = tokens.astype(f32)
    norm_one, pull_one = jax.vjp(layer_norm, x_float, ln1_g.astype(f32), ln1_b.astype(f32))
    normed = norm_one.astype(bf16)
    joined = jnp.dot(normed, w_qkv, preferred_element_type=f32) + b_qkv.astype(f32)
    queries = rotate(joined[:, :model_width], positions, 1.0).astype(bf16)
    keys_rot = rotate(joined[:, model_width : 2 * model_width], positions, 1.0).astype(bf16)
    values_in = joined[:, 2 * model_width :].astype(bf16)
    q_heads, k_heads, v_heads = (
        lax.all_to_all(queries, "ulysses", split_axis=1, concat_axis=0, tiled=True),
        lax.all_to_all(keys_rot, "ulysses", split_axis=1, concat_axis=0, tiled=True),
        lax.all_to_all(values_in, "ulysses", split_axis=1, concat_axis=0, tiled=True),
    )
    block_len = min(512, head_rows)
    q_blocks = head_rows // block_len
    q_grid = q_heads.reshape(q_blocks, block_len, local_heads, HEAD)
    place_grid = head_places.reshape(q_blocks, block_len)
    start_state = (
        jnp.full((q_blocks, local_heads, block_len), BIG_NEG, f32),
        jnp.zeros((q_blocks, local_heads, block_len), f32),
        jnp.zeros((q_blocks, block_len, local_heads, HEAD), f32),
    )
    state = start_state
    key_piece = lax.all_gather(k_heads, "blk", axis=0, tiled=True)
    value_piece = lax.all_gather(v_heads, "blk", axis=0, tiled=True)
    count = key_piece.shape[0]
    span_len = min(count, head_rows)
    for j in range(count // span_len):
        key_block = key_piece[j * span_len : (j + 1) * span_len].reshape(
            span_len, local_heads, HEAD
        )
        value_block = value_piece[j * span_len : (j + 1) * span_len].reshape(
            span_len, local_heads, HEAD
        )
        block_places = order_all[j * span_len : (j + 1) * span_len]

        def update(item):
            query_block, query_places, run_max, run_sum, run_acc = item
            scores = (
                jnp.einsum("qhd,khd->hqk", query_block, key_block, preferred_element_type=f32)
                * scale
            )
            allowed = (block_places[None, :] <= query_places[:, None])[None]
            scores = jnp.where(allowed, scores, BIG_NEG)
            new_max = jnp.maximum(run_max, jnp.max(scores, -1))
            weights = jnp.where(allowed, jnp.exp(scores - new_max[..., None]), 0.0)
            factor = jnp.exp(run_max - new_max)
            run_sum = run_sum * factor + jnp.sum(weights, -1)
            run_acc = run_acc * factor.T[:, :, None] + jnp.einsum(
                "hqk,khd->qhd", weights.astype(bf16), value_block, preferred_element_type=f32
            )
            return (new_max, run_sum, run_acc)

        state = lax.map(update, (q_grid, place_grid) + tuple(state))
    run_max, run_sum, run_acc = state
    log_total = run_max + jnp.log(run_sum)
    attended = run_acc / run_sum.transpose(0, 2, 1)[..., None]
    mixed_heads = attended.astype(bf16).reshape(head_rows, local_cols)
    mixed = lax.all_to_all(mixed_heads, "ulysses", split_axis=0, concat_axis=1, tiled=True)
    attn_out = jnp.dot(mixed, w_out, preferred_element_type=f32) + b_out.astype(f32)
    norm_two, pull_two = jax.vjp(layer_norm, x_float, ln2_g.astype(f32), ln2_b.astype(f32))
    normed_two = norm_two.astype(bf16)
    hidden = jnp.dot(normed_two, w_up, preferred_element_type=f32) + b_up.astype(f32)
    active_f, pull_gelu = jax.vjp(gelu_exact, hidden)
    active = active_f.astype(bf16)
    mlp_out = jnp.dot(active, w_down, preferred_element_type=f32) + b_down.astype(f32)
    output = (x_float + attn_out + mlp_out).astype(bf16)
    grad_float = cotangent.astype(f32)
    g_down = jnp.einsum("tf,td->fd", active, cotangent, preferred_element_type=f32)
    g_down_bias = jnp.sum(grad_float, 0)
    d_active = jnp.einsum("td,fd->tf", cotangent, w_down, preferred_element_type=f32)
    d_hidden = pull_gelu(d_active)[0].astype(bf16)
    g_up_bias = jnp.sum(d_hidden.astype(f32), 0)
    g_up = jnp.einsum("td,tf->df", normed_two, d_hidden, preferred_element_type=f32)
    d_norm_two = jnp.einsum("tf,df->td", d_hidden, w_up, preferred_element_type=f32)
    d_x_two, g_ln2_g, g_ln2_b = pull_two(d_norm_two)
    mlp_grads = (g_ln2_g, g_ln2_b, g_up, g_up_bias, g_down, g_down_bias)
    g_out = jnp.einsum("te,td->ed", mixed, cotangent, preferred_element_type=f32)
    d_mixed = jnp.einsum("td,ed->te", cotangent, w_out, preferred_element_type=f32).astype(bf16)
    d_heads = lax.all_to_all(d_mixed, "ulysses", split_axis=1, concat_axis=0, tiled=True)
    key_all, value_all = (
        lax.all_gather(k_heads, "blk", axis=0, tiled=True),
        lax.all_gather(v_heads, "blk", axis=0, tiled=True),
    )
    d_grid = d_heads.reshape(q_blocks, block_len, local_heads, HEAD)
    delta = jnp.sum(d_grid.astype(f32) * attended, -1).transpose(0, 2, 1)
    key_count = seq_len // head_rows
    key_grid = key_all.reshape(key_count, head_rows, local_heads, HEAD)
    value_grid = value_all.reshape(key_count, head_rows, local_heads, HEAD)
    key_place_grid = order_all.reshape(key_count, head_rows)
    empty = jnp.zeros((head_rows, local_heads, HEAD), f32)

    def key_step(d_query, key_item):
        key_block, value_block, block_places = key_item

        def query_step(kv_sums, query_item):
            query_block, grad_block, query_places, block_total, block_delta = query_item
            probs, d_scores = score_grads(
                query_block,
                grad_block,
                query_places,
                block_total,
                block_delta,
                key_block,
                value_block,
                block_places,
            )
            d_values = jnp.einsum(
                "hqk,qhd->khd", probs.astype(bf16), grad_block, preferred_element_type=f32
            )
            d_q = (
                jnp.einsum("hqk,khd->qhd", d_scores, key_block, preferred_element_type=f32) * scale
            )
            d_k = (
                jnp.einsum("hqk,qhd->khd", d_scores, query_block, preferred_element_type=f32)
                * scale
            )
            return ((kv_sums[0] + d_k, kv_sums[1] + d_values), d_q)

        kv_sums, d_adds = lax.scan(
            query_step, (empty, empty), (q_grid, d_grid, place_grid, log_total, delta)
        )
        return (d_query + d_adds, kv_sums)

    d_query, (d_key_all, d_value_all) = lax.scan(
        key_step, jnp.zeros(q_grid.shape, f32), (key_grid, value_grid, key_place_grid)
    )
    d_key_mine, d_value_mine = (
        lax.psum_scatter(
            d_key_all.reshape(seq_len, local_cols).astype(jnp.bfloat16),
            "blk",
            scatter_dimension=0,
            tiled=True,
        ).astype(jnp.float32),
        lax.psum_scatter(
            d_value_all.reshape(seq_len, local_cols).astype(jnp.bfloat16),
            "blk",
            scatter_dimension=0,
            tiled=True,
        ).astype(jnp.float32),
    )
    d_query_rows = rotate(d_query.reshape(head_rows, local_cols), head_places, -1.0).astype(bf16)
    d_key_rows = rotate(d_key_mine, head_places, -1.0).astype(bf16)
    d_value_rows = d_value_mine.astype(bf16)
    d_q_seq, d_k_seq, d_v_seq = (
        lax.all_to_all(d_query_rows, "ulysses", split_axis=0, concat_axis=1, tiled=True),
        lax.all_to_all(d_key_rows, "ulysses", split_axis=0, concat_axis=1, tiled=True),
        lax.all_to_all(d_value_rows, "ulysses", split_axis=0, concat_axis=1, tiled=True),
    )
    d_joined = jnp.concatenate([d_q_seq, d_k_seq, d_v_seq], 1)
    g_qkv_bias = jnp.sum(d_joined.astype(f32), 0)
    g_qkv = jnp.einsum("td,te->de", normed, d_joined, preferred_element_type=f32)
    d_norm_one = jnp.einsum("te,de->td", d_joined, w_qkv, preferred_element_type=f32)
    d_x_one, g_ln1_g, g_ln1_b = pull_one(d_norm_one)
    input_grad = (grad_float + d_x_one + d_x_two).astype(bf16)
    attn_grads = (g_ln1_g, g_ln1_b, g_qkv, g_qkv_bias, g_out, g_down_bias)
    shards = jax.tree.map(
        lambda part: part.astype(jnp.float32),
        lax.psum_scatter(
            shortened(attn_grads + mlp_grads), "fsdp", scatter_dimension=0, tiled=True
        ),
    )
    summed = jax.tree.map(
        lambda part: part.astype(jnp.float32), lax.psum(shortened(shards), ("blk", "ulysses"))
    )
    return (
        output,
        input_grad,
        summed[0],
        summed[1],
        summed[6],
        summed[7],
        summed[2],
        summed[3],
        summed[4],
        summed[5],
        summed[8],
        summed[9],
        summed[10],
        summed[11],
    )


def solution(mesh):
    return jax.shard_map(
        on_device,
        mesh=mesh,
        in_specs=(
            P(("fsdp", "blk", "ulysses"), None),
            P(("fsdp", "blk", "ulysses")),
            P(("fsdp", "blk", "ulysses"), None),
            P("fsdp"),
            P("fsdp"),
            P("fsdp"),
            P("fsdp"),
            P("fsdp", None),
            P("fsdp"),
            P("fsdp", None),
            P("fsdp"),
            P("fsdp", None),
            P("fsdp"),
            P("fsdp", None),
            P("fsdp"),
        ),
        out_specs=(
            P(("fsdp", "blk", "ulysses"), None),
            P(("fsdp", "blk", "ulysses"), None),
            P("fsdp"),
            P("fsdp"),
            P("fsdp"),
            P("fsdp"),
            P("fsdp", None),
            P("fsdp"),
            P("fsdp", None),
            P("fsdp"),
            P("fsdp", None),
            P("fsdp"),
            P("fsdp", None),
            P("fsdp"),
        ),
        check_vma=False,
    )
```

profile of v0, /device:TPU:9, one launch (start us, length us, event | category | flops | bytes accessed | tf_op | source)
XLA Modules:
  0.0 824.8 jit_solution(3267084564318168229)
XLA Ops:
  21.7 38.5 %all-gather.16.cloned.1.call-done = bf16[768,2304]{1,0:T(8,128)(2,1)} async-done(((bf16[384,2304]{1,0:T(8,128)(2,1)}), bf16[768,2304]{1,0:T(8,128)(2,1)}) %all-gather.16.cloned.1.call-update) | async-done | bytes 3538960 | tf_op jit(solution)/shard_map/all_gather | solution.py:92
  66.3 12.8 %all_to_all.134 = bf16[256,4,192]{0,2,1:T(8,128)(2,1)S(1)} all-to-all(bf16[256,4,192]{0,2,1:T(8,128)(2,1)S(1)} %bitcast.496), channel_id=1, replica_groups=mesh['fsdp'=2,'blk'=4,'ulysses'=4] {'ulysses'}, dimensions={1} | all-to-all | bytes 786432 | tf_op jit(solution)/shard_map/all_to_all | solution.py:121
  81.4 13.8 %all_to_all.135 = bf16[256,4,192]{0,2,1:T(8,128)(2,1)S(1)} all-to-all(bf16[256,4,192]{0,2,1:T(8,128)(2,1)S(1)} %bitcast.490), channel_id=1, replica_groups=mesh['fsdp'=2,'blk'=4,'ulysses'=4] {'ulysses'}, dimensions={1} | all-to-all | bytes 786432 | tf_op jit(solution)/shard_map/all_to_all | solution.py:122
  98.5 13.8 %all_to_all.136 = bf16[256,4,192]{0,2,1:T(8,128)(2,1)S(1)} all-to-all(bf16[256,4,192]{0,2,1:T(8,128)(2,1)S(1)} %bitcast.492), channel_id=1, replica_groups=mesh['fsdp'=2,'blk'=4,'ulysses'=4] {'ulysses'}, dimensions={1} | all-to-all | bytes 786432 | tf_op jit(solution)/shard_map/all_to_all | solution.py:190
  112.3 5.5 all-to-all-start
  118.5 30.2 %all-gather = s32[16,1,256]{2,1,0:T(1,128)S(1)} all-gather(s32[1,1,256]{2,1,0:T(1,128)S(1)} %bitcast.516), channel_id=1, replica_groups=mesh['fsdp'=2,'blk'=4,'ulysses'=4] {'blk','ulysses'}, dimensions={0}, use_global_device_ids=true | all-gather | bytes 17408 | tf_op jit(solution)/shard_map/all_gather | solution.py:109
  156.9 14.8 %while.94 = (s32[]{:T(128)}, f32[2,3,512]{2,1,0:T(4,128)S(1)}, f32[2,3,512]{2,1,0:T(4,128)S(1)}, f32[2,512,3,64]{1,3,2,0:T(8,128)S(1)}, s32[1024]{0:T(1024)S(1)}...) while((s32[]{:T(128)}, f32[2,3,512]{2,1,0:T(4,128)S(1)}, ...), condition=%wide.region_5.6_spmd.clone, body=%wide.region_2.5_spmd.sunk.clone | while | flops 423730688 | bytes 24017040 | solution.py:164
  172.7 16.4 %while.95 = (s32[]{:T(128)}, f32[2,3,512]{2,1,0:T(4,128)S(1)}, f32[2,3,512]{2,1,0:T(4,128)S(1)}, f32[2,512,3,64]{1,3,2,0:T(8,128)}, f32[2,3,512]{2,1,0:T(4,128)S...) while((s32[]{:T(128)}, f32[2,3,512]{2,1,0:T(4,128)S(1)}, ...), condition=%wide.region_9.10_spmd.clone, body=%wide.region_6.9_spmd.sunk.clone | while | flops 423827456 | bytes 30724324 | solution.py:164
  189.2 14.7 %while.96 = (s32[]{:T(128)}, f32[2,3,512]{2,1,0:T(4,128)S(1)}, f32[2,3,512]{2,1,0:T(4,128)S(1)}, f32[2,512,3,64]{1,3,2,0:T(8,128)S(1)}, f32[2,3,512]{2,1,0:T(4,1...) while((s32[]{:T(128)}, f32[2,3,512]{2,1,0:T(4,128)S(1)}, ...), condition=%wide.region_13.14_spmd.clone, body=%wide.region_10.13_spmd.sunk.clone | while | flops 423827456 | bytes 27578568 | solution.py:164
  204.7 23.1 %while.97 = (s32[]{:T(128)}, f32[2,3,512]{2,1,0:T(4,128)S(1)}, f32[2,3,512]{2,1,0:T(4,128)S(1)}, f32[2,512,3,64]{1,0,3,2:T(2,128)S(1)}, f32[2,3,512]{2,1,0:T(4,1...) while((s32[]{:T(128)}, f32[2,3,512]{2,1,0:T(4,128)S(1)}, ...), condition=%wide.region_17.18_spmd.clone, body=%wide.region_14.17_spmd.sunk.clone | while | flops 423827456 | bytes 29147340 | solution.py:164
  240.1 145.2 %while.99 = (s32[]{:T(128)}, f32[2,512,3,64]{1,3,2,0:T(8,128)}, bf16[4,1024,3,64]{1,3,2,0:T(8,128)(2,1)}, bf16[4,1024,3,64]{1,3,2,0:T(8,128)(2,1)}, bf16[4,1024,...) while((s32[]{:T(128)}, f32[2,512,3,64]{1,3,2,0:T(8,128)}, ...), condition=%wide.region_22.23_spmd.clone.clone, body=%wide.region_19.22_spmd.clone.sunk.clone | while | flops 1027506176 | bytes 129663816 | solution.py:235
  242.3 29.5 %while.98 = (s32[]{:T(128)}, f32[1024,3,64]{0,2,1:T(8,128)}, f32[1024,3,64]{0,2,1:T(8,128)}, f32[2,512,3,64]{1,3,2,0:T(8,128)}, bf16[2,512,3,64]{1,3,2,0:T(8,128...) while((s32[]{:T(128)}, f32[1024,3,64]{0,2,1:T(8,128)}, ...), condition=%wide.region_21.21_spmd.clone, body=%wide.region_20.20_spmd.clone.sunk | while | flops 1027112960 | bytes 97411504 | solution.py:230
  265.5 4.3 fusion.309
  278.3 29.5 %while.98 = (s32[]{:T(128)}, f32[1024,3,64]{0,2,1:T(8,128)}, f32[1024,3,64]{0,2,1:T(8,128)}, f32[2,512,3,64]{1,3,2,0:T(8,128)}, bf16[2,512,3,64]{1,3,2,0:T(8,128...) while((s32[]{:T(128)}, f32[1024,3,64]{0,2,1:T(8,128)}, ...), condition=%wide.region_21.21_spmd.clone, body=%wide.region_20.20_spmd.clone.sunk | while | flops 1027112960 | bytes 97411504 | solution.py:230
  301.5 4.3 fusion.309
  314.6 29.5 %while.98 = (s32[]{:T(128)}, f32[1024,3,64]{0,2,1:T(8,128)}, f32[1024,3,64]{0,2,1:T(8,128)}, f32[2,512,3,64]{1,3,2,0:T(8,128)}, bf16[2,512,3,64]{1,3,2,0:T(8,128...) while((s32[]{:T(128)}, f32[1024,3,64]{0,2,1:T(8,128)}, ...), condition=%wide.region_21.21_spmd.clone, body=%wide.region_20.20_spmd.clone.sunk | while | flops 1027112960 | bytes 97411504 | solution.py:230
  337.8 4.3 fusion.309
  350.8 29.5 %while.98 = (s32[]{:T(128)}, f32[1024,3,64]{0,2,1:T(8,128)}, f32[1024,3,64]{0,2,1:T(8,128)}, f32[2,512,3,64]{1,3,2,0:T(8,128)}, bf16[2,512,3,64]{1,3,2,0:T(8,128...) while((s32[]{:T(128)}, f32[1024,3,64]{0,2,1:T(8,128)}, ...), condition=%wide.region_21.21_spmd.clone, body=%wide.region_20.20_spmd.clone.sunk | while | flops 1027112960 | bytes 97411504 | solution.py:230
  403.5 5.1 all-to-all-start.3
  408.9 5.5 convolution_add_fusion.1
  416.8 12.0 %fusion.182 = (bf16[3072]{0:T(1024)(128)(2,1)}, bf16[256,3072]{1,0:T(8,128)(2,1)S(1)}, f32[256,3072]{1,0:T(8,128)}) fusion(f32[256,3072]{1,0:T(8,128)} %convolution_add_fusion.1, bf16[256,768]{1,0:T(8,128)(2,1)S(1)} %copy-done.9, bf16[3072,768]{1,0:T(8,128)(2,1)} %all-gather.26.cloned.1.call-done), kind=kOutput, calls=%fused_computation.254 | convolution fusion | flops 1265366016 | bytes 12982272 | tf_op jit(solution)/shard_map/td,fd->tf/dot_general | solution.py:181
  441.6 5.3 all-to-all-start.7
  454.8 4.6 all-to-all-start.6
  461.7 4.3 all-to-all-done.6
  466.0 12.4 %all_to_all.137 = bf16[4,256,192]{1,2,0:T(8,128)(2,1)S(1)} all-to-all(bf16[4,256,192]{1,2,0:T(8,128)(2,1)S(1)} %copy.100), channel_id=1, replica_groups=mesh['fsdp'=2,'blk'=4,'ulysses'=4] {'ulysses'}, dimensions={0} | all-to-all | bytes 786432 | tf_op jit(solution)/shard_map/all_to_all | solution.py:256
  478.4 4.4 convolution_convert_fusion.2
  482.9 54.6 %reduce-scatter.15.cloned.1.call-done = bf16[384,3072]{1,0:T(8,128)(2,1)} async-done(((bf16[768,3072]{1,0:T(8,128)(2,1)}), bf16[384,3072]{1,0:T(8,128)(2,1)}) %reduce-scatter.15.cloned.1.call-update) | async-done | bytes 2359312 | tf_op jit(solution)/shard_map/reduce_scatter | solution.py:269
  537.5 62.9 %reduce-scatter.17.cloned.1.call-done = bf16[1536,768]{1,0:T(8,128)(2,1)} async-done(((bf16[3072,768]{1,0:T(8,128)(2,1)}), bf16[1536,768]{1,0:T(8,128)(2,1)}) %reduce-scatter.17.cloned.1.call-update) | async-done | bytes 2359312 | tf_op jit(solution)/shard_map/reduce_scatter | solution.py:269
  600.4 50.5 %reduce-scatter.11.cloned.1.call-done = bf16[384,2304]{1,0:T(8,128)(2,1)} async-done(((bf16[768,2304]{1,0:T(8,128)(2,1)}), bf16[384,2304]{1,0:T(8,128)(2,1)}) %reduce-scatter.11.cloned.1.call-update) | async-done | bytes 1769488 | tf_op jit(solution)/shard_map/reduce_scatter | solution.py:269
  676.7 6.3 all-reduce.9
  683.5 59.2 %all-reduce.7 = (bf16[384]{0:T(512)(128)(2,1)S(1)}, bf16[384]{0:T(512)(128)(2,1)S(1)}, bf16[384]{0:T(512)(128)(2,1)S(1)}, bf16[384]{0:T(512)(128)(2,1)S(1)}, bf1...) all-reduce(bf16[384]{0:T(512)(128)(2,1)S(1)} %dynamic-slice.1, ...), channel_id=1, replica_groups=mesh['fsdp'=2,'blk'=4,'ulysses'=4] {'blk','ulysses'}, use_global_device_ids=true, to_apply=%region_31.32 | all-reduce | flops 4608 | bytes 18432 | tf_op jit(solution)/shard_map/psum | solution.py:274
  747.5 59.9 %all-reduce.12.cloned.1.call-done = (bf16[384,2304]{1,0:T(8,128)(2,1)}, bf16[384,768]{1,0:T(8,128)(2,1)}, bf16[384,3072]{1,0:T(8,128)(2,1)}, bf16[1536,768]{1,0:T(8,128)(2,1)}) async-done(((bf16[384,2304]{1,0:T(8,128)(2,1)}, bf16[384,768]{1,0:T(8,128)(2,1)}, bf16[384,3072]{1,0:T(8,128)(2,1)}, bf16[1536,768]{1,0:T(8,128)(2,1)}), (bf16[384,2304]{1,0:T(8,128)(2,1)}, bf16[384,768]{1,0:T(8,128)(2,1)}, ...) | async-done | bytes 7077904 | tf_op jit(solution)/shard_map/psum | solution.py:274
  (647 shorter events, 330.6 us)
Async XLA Ops:
  7.2 53.0 %copy-start.6 = (bf16[256,768]{1,0:T(8,128)(2,1)S(1)}, bf16[256,768]{1,0:T(8,128)(2,1)}, u32[]{:S(2)}) copy-start(bf16[256,768]{1,0:T(8,128)(2,1)} %param.27) | copy-start | bytes 1179652
  7.2 14.3 %copy-start.62 = (s32[256]{0:T(256)S(1)}, s32[256]{0:T(256)}, u32[]{:S(2)}) copy-start(s32[256]{0:T(256)} %param.28) | copy-start | bytes 3076
  7.2 53.0 %all-gather.16.cloned.1.call-start = ((), (), s32[]{:S(2)}) async-start(), calls=%async_computation.14 | async-start | bytes 5308416 | tf_op jit(solution)/shard_map/all_gather | solution.py:92
  8.0 88.6 %all-gather.22.cloned.1.call-start = ((), (), s32[]{:S(2)}) async-start(), calls=%async_computation.17 | async-start | bytes 1769472 | tf_op jit(solution)/shard_map/all_gather | solution.py:94
  8.7 144.1 %all-gather.18.cloned.1.call-start = ((), (), s32[]{:S(2)}) async-start(), calls=%async_computation.15 | async-start | bytes 1966080 | tf_op jit(solution)/shard_map/all_gather | solution.py:134
  8.8 54.6 %copy-start.65 = (f32[8]{0:T(128)}, f32[8]{0:T(128)S(1)}, u32[]{:S(2)}) copy-start(f32[8]{0:T(128)S(1)} %multiply_power_fusion) | copy-start | bytes 100
  9.9 50.3 %copy-start.49 = (f32[256]{0:T(256)}, f32[256]{0:T(256)S(1)}, u32[]{:S(2)}) copy-start(f32[256]{0:T(256)S(1)} %broadcast_multiply_fusion) | copy-start | bytes 3076
  11.8 48.4 %copy-start.51 = (f32[256]{0:T(256)}, f32[256]{0:T(256)S(1)}, u32[]{:S(2)}) copy-start(f32[256]{0:T(256)S(1)} %fusion.171) | copy-start | bytes 3076
  18.3 41.9 %copy-start.60 = (f32[768]{0:T(1024)}, f32[768]{0:T(1024)S(1)}, u32[]{:S(2)}) copy-start(f32[768]{0:T(1024)S(1)} %reshape.537) | copy-start | bytes 9220
  21.5 38.7 %copy-start.47 = (f32[768]{0:T(1024)}, f32[768]{0:T(1024)S(1)}, u32[]{:S(2)}) copy-start(f32[768]{0:T(1024)S(1)} %reshape.536) | copy-start | bytes 9220
  79.9 16.7 %copy-start.8 = (bf16[256,768]{1,0:T(8,128)(2,1)S(1)}, bf16[256,768]{1,0:T(8,128)(2,1)}, u32[]{:S(2)}) copy-start(bf16[256,768]{1,0:T(8,128)(2,1)} %param.29) | copy-start | bytes 1179652
  79.9 74.4 %all-gather.20.cloned.1.call-start = ((), (), s32[]{:S(2)}) async-start(), calls=%async_computation.16 | async-start | bytes 1966080 | tf_op jit(solution)/shard_map/all_gather | solution.py:135
  95.9 312.9 %all-gather.24.cloned.1.call-start = ((), (), s32[]{:S(2)}) async-start(), calls=%async_computation.18 | async-start | bytes 7077888 | tf_op jit(solution)/shard_map/all_gather | solution.py:96
  112.3 39.2 %all-to-all-start = ((bf16[256,4,192]{0,2,1:T(8,128)(2,1)}), bf16[256,4,192]{0,2,1:T(8,128)(2,1)S(1)}, u32[]{:S(2)}, u32[]{:S(2)}) async-start(bf16[256,4,192]{0,2,1:T(8,128)(2,1)} %bitcast.38), calls=%async_computation | async-start | bytes 786432 | tf_op jit(solution)/shard_map/all_to_all | solution.py:120
  117.8 298.9 %all-gather.26.cloned.1.call-start = ((), (), s32[]{:S(2)}) async-start(), calls=%async_computation.19 | async-start | bytes 7077888 | tf_op jit(solution)/shard_map/all_gather | solution.py:98
  118.4 321.3 %reduce-scatter.9.cloned.1.call-start = ((), (), s32[]{:S(2)}) async-start(), calls=%async_computation.21 | async-start | bytes 1966080 | tf_op jit(solution)/shard_map/reduce_scatter | solution.py:245
  204.7 24.0 %copy-start.15 = (bf16[4096,192]{0,1:T(8,128)(2,1)S(1)}, bf16[4096,192]{0,1:T(8,128)(2,1)}, u32[]{:S(2)}) copy-start(bf16[4096,192]{0,1:T(8,128)(2,1)} %all-gather.18.cloned.1.call-done) | copy-start | bytes 4718596
  389.7 60.3 %reduce-scatter.7.cloned.1.call-start = ((), (), s32[]{:S(2)}) async-start(), calls=%async_computation.20 | async-start | bytes 1966080 | tf_op jit(solution)/shard_map/reduce_scatter | solution.py:239
  391.0 11.5 %copy-start.26 = (bf16[2,512,3,64]{1,0,3,2:T(2,128)(2,1)S(1)}, bf16[2,512,3,64]{1,0,3,2:T(2,128)(2,1)}, u32[]{:S(2)}) copy-start(bf16[2,512,3,64]{1,0,3,2:T(2,128)(2,1)} %get-tuple-element.843) | copy-start | bytes 1179652
  391.0 17.8 %copy-start.7 = (bf16[256,768]{1,0:T(8,128)(2,1)S(1)}, bf16[256,768]{1,0:T(8,128)(2,1)}, u32[]{:S(2)}) copy-start(bf16[256,768]{1,0:T(8,128)(2,1)} %param.27) | copy-start | bytes 1179652
  391.0 17.8 %copy-start.50 = (f32[256]{0:T(256)S(1)}, f32[256]{0:T(256)}, u32[]{:S(2)}) copy-start(f32[256]{0:T(256)} %copy-done.49) | copy-start | bytes 3076
  391.1 17.8 %copy-start.52 = (f32[256]{0:T(256)S(1)}, f32[256]{0:T(256)}, u32[]{:S(2)}) copy-start(f32[256]{0:T(256)} %copy-done.51) | copy-start | bytes 3076
  403.5 11.7 %all-to-all-start.3 = ((bf16[4,256,192]{1,2,0:T(8,128)(2,1)}), bf16[4,256,192]{1,2,0:T(8,128)(2,1)S(1)}, u32[]{:S(2)}, u32[]{:S(2)}) async-start(bf16[4,256,192]{1,2,0:T(8,128)(2,1)} %copy.91), calls=%async_computation.3 | async-start | bytes 786432 | tf_op jit(solution)/shard_map/all_to_all | solution.py:169
  408.6 74.3 %reduce-scatter.13.cloned.1.call-start = ((), (), s32[]{:S(2)}) async-start(), calls=%async_computation.23 | async-start | bytes 1769472 | tf_op jit(solution)/shard_map/reduce_scatter | solution.py:269
  416.7 120.8 %reduce-scatter.15.cloned.1.call-start = ((), (), s32[]{:S(2)}) async-start(), calls=%async_computation.24 | async-start | bytes 7077888 | tf_op jit(solution)/shard_map/reduce_scatter | solution.py:269
  432.6 167.8 %reduce-scatter.17.cloned.1.call-start = ((), (), s32[]{:S(2)}) async-start(), calls=%async_computation.25 | async-start | bytes 7077888 | tf_op jit(solution)/shard_map/reduce_scatter | solution.py:269
  441.6 13.2 %all-to-all-start.7 = ((bf16[4,256,192]{1,2,0:T(8,128)(2,1)}), bf16[4,256,192]{1,2,0:T(8,128)(2,1)}, u32[]{:S(2)}, u32[]{:S(2)}) async-start(bf16[4,256,192]{1,2,0:T(8,128)(2,1)} %bitcast.488), calls=%async_computation.9 | async-start | bytes 786432 | tf_op jit(solution)/shard_map/all_to_all | solution.py:258
  453.7 24.7 %copy-start.48 = (f32[768]{0:T(1024)S(1)}, f32[768]{0:T(1024)}, u32[]{:S(2)}) copy-start(f32[768]{0:T(1024)} %copy-done.47) | copy-start | bytes 9220
  454.8 11.2 %all-to-all-start.6 = ((bf16[4,256,192]{1,2,0:T(8,128)(2,1)}), bf16[4,256,192]{1,2,0:T(8,128)(2,1)}, u32[]{:S(2)}, u32[]{:S(2)}) async-start(bf16[4,256,192]{1,2,0:T(8,128)(2,1)} %copy.102), calls=%async_computation.7 | async-start | bytes 786432 | tf_op jit(solution)/shard_map/all_to_all | solution.py:257
  459.4 191.5 %reduce-scatter.11.cloned.1.call-start = ((), (), s32[]{:S(2)}) async-start(), calls=%async_computation.22 | async-start | bytes 5308416 | tf_op jit(solution)/shard_map/reduce_scatter | solution.py:269
  482.8 324.5 %all-reduce.12.cloned.1.call-start = ((), (), s32[]{:S(2)}) async-start(), calls=%async_computation.26 | async-start | bytes 14155776 | tf_op jit(solution)/shard_map/psum | solution.py:274
  745.6 71.8 %copy-start.58 = (f32[384]{0:T(512)}, f32[384]{0:T(512)S(1)}, u32[]{:S(2)}) copy-start(f32[384]{0:T(512)S(1)} %convert_element_type.249) | copy-start | bytes 4612
  (142 other events, 419.3 us)
Sparse Core Ops, SparseCore 0:
  9.6 50.5 all-gather.15
  61.7 22.7 all-gather.21
  86.7 20.0 all-gather.17
  108.8 19.6 all-gather.19
  129.9 62.2 all-gather.23
  193.6 62.6 all-gather.25
  389.8 29.1 reduce-scatter.8
  421.7 28.2 reduce-scatter.6
  452.8 21.7 reduce-scatter.12
  477.4 59.9 reduce-scatter.14
  540.4 59.9 reduce-scatter.16
  603.2 47.6 reduce-scatter.10
  654.9 152.4 all-reduce.11
where the time goes:
time: 834 us; the launch traced here: 825 us
  waiting for transfers between devices  275 us (33%)
  matrix products  187 us (22%)
  blocking collectives  174 us (21%)
  local copies, waits for them, and re-layouts  81.4 us (10%)
  other arithmetic  66.8 us (8%)
  starting transfers between devices  21.1 us (3%)
  between operations  17.1 us (2%)
    reduce_scatter x4, waiting for transfers between devices, on_device(): lax.psum_scatter(shortened(attn_grads + mlp_grads), 'fsdp', scatter_dimen...  168 us
    psum x1, waiting for transfers between devices, on_device(): lax.psum(shortened(shards), ('blk', 'ulysses'))  59.9 us
    psum x1, blocking collectives, on_device(): lax.psum(shortened(shards), ('blk', 'ulysses'))  59.2 us
    all_gather x1, waiting for transfers between devices, on_device(): lax.all_gather(qkv_weight, 'fsdp', axis=0, tiled=True)  38.5 us
    dot_general x8, matrix products, query_step(): jnp.einsum('hqk,qhd->khd', probs.astype(bf16), grad_block, preferred_elem...  33.4 us
    all_gather x1, blocking collectives, on_device(): lax.all_gather(positions, ('blk', 'ulysses'), axis=0, tiled=True)  30.2 us
    dot_general x8, matrix products, score_grads(): jnp.einsum('qhd,khd->hqk', grad_block, value_block, preferred_element_typ...  22.6 us
    dot_general x8, matrix products, query_step(): jnp.einsum('hqk,qhd->khd', d_scores, query_block, preferred_element_type=...  22.3 us
  transfers between devices with their start and end apart: 17, of which 8 were waited for; matrix products, arithmetic and copies ran while one was open for 37% of the time, Pallas kernels for 0%

commit v1 on v0

v1 whole, which is shorter than its diff:
```python
import jax
import jax.numpy as jnp
from jax import lax
from jax.experimental import pallas as pl
from jax.experimental.pallas import tpu as pltpu
from jax.sharding import PartitionSpec as P

HEAD = 64
ROT = 16
STRETCH = 128
CHUNK = 2
BIG_NEG = -1e30

f32 = jnp.float32
bf16 = jnp.bfloat16


def layer_norm(values, gain, shift):
    center = jnp.mean(values, -1, keepdims=True)
    offset = values - center
    spread = jnp.mean(offset * offset, -1, keepdims=True)
    return offset * lax.rsqrt(spread + 1e-05) * gain + shift


def gelu_exact(values):
    return jax.nn.gelu(values, approximate=False)


def swap(values, axis, bits):
    count = lax.axis_size(axis)
    return lax.ppermute(values, axis, [(i, i ^ bits) for i in range(count)])


def bit_of(axis, bit):
    return (lax.axis_index(axis) // bit) % 2


def in_order(bit, mine, other, axis=0):
    return jnp.concatenate([jnp.where(bit == 0, mine, other), jnp.where(bit == 0, other, mine)], axis)


def by_device(pieces, index):
    step = 1
    while step < len(pieces):
        odd = (index // step) % 2 == 1
        pieces = [jnp.where(odd, pieces[i ^ step], pieces[i]) for i in range(len(pieces))]
        step *= 2
    return pieces


def add_half(halves, axis, bit):
    which = bit_of(axis, bit)
    got = swap(jnp.where(which == 0, halves[1], halves[0]), axis, bit)
    kept = jnp.where(which == 0, halves[0], halves[1])
    return (kept.astype(f32) + got.astype(f32)).astype(bf16)


def halves_of(values, axis):
    half = values.shape[axis] // 2
    return (
        lax.slice_in_dim(values, 0, half, axis=axis),
        lax.slice_in_dim(values, half, 2 * half, axis=axis),
    )


def share_half(values, axis, bit, dim):
    return in_order(bit_of(axis, bit), values, swap(values, axis, bit), dim)


def gather_small(shard):
    if lax.axis_size("fsdp") != 2:
        return lax.all_gather(shard[None], "fsdp", axis=0, tiled=True)
    return in_order(lax.axis_index("fsdp"), shard[None], swap(shard[None], "fsdp", 1))


def other_rows(shard):
    quarter = shard.shape[0] // 4
    place = bit_of("blk", 1) * 2 + bit_of("blk", 2)
    part = swap(lax.dynamic_slice_in_dim(shard, place * quarter, quarter), "fsdp", 1)
    return share_half(share_half(part, "blk", 2, 0), "blk", 1, 0)


def gather_rows(shard):
    if lax.axis_size("fsdp") != 2:
        return lax.all_gather(shard, "fsdp", axis=0, tiled=True)
    return in_order(lax.axis_index("fsdp"), shard, other_rows(shard))


def attend_kernel(rank, q_ref, g_ref, kv_ref, o_ref, dq_ref, dkv_ref, rows, lanes, sums, probs, order):
    n_keys = rank.shape[0]
    own = q_ref.shape[-1] // STRETCH
    wide = 2 * STRETCH
    span = CHUNK * STRETCH

    for t in range(n_keys):
        i, at = t // own, (t % own) * STRETCH
        both = jnp.concatenate(
            [kv_ref[i, 0, :, at : at + STRETCH], kv_ref[i, 1, :, at : at + STRETCH]], 0
        )
        place = rank[t]
        lanes[place] = both
        rows[place] = both.T
    sums[...] = jnp.zeros_like(sums)
    for a in range(own):
        before = jnp.int32(0)
        for b in range(own):
            before += (rank[b] < rank[a]).astype(jnp.int32)
        order[before] = a

    def side(j, part):
        return jnp.concatenate(
            [lanes[j * CHUNK + i, part * HEAD : (part + 1) * HEAD, :] for i in range(CHUNK)], 1
        )

    def keys(j):
        return rows[pl.ds(j * CHUNK, CHUNK)].reshape(span, 2 * HEAD)

    def pair(p, carry):
        a, b = order[2 * p], order[2 * p + 1]
        ra, rb = rank[a], rank[b]
        at_a = pl.ds(pl.multiple_of(a * STRETCH, STRETCH), STRETCH)
        at_b = pl.ds(pl.multiple_of(b * STRETCH, STRETCH), STRETCH)
        q = jnp.concatenate([q_ref[:, at_a], q_ref[:, at_b]], 1)
        g = jnp.concatenate([g_ref[:, at_a], g_ref[:, at_b]], 1)
        none = jnp.zeros_like(q)
        q_low = jnp.concatenate([q, none], 0)
        g_high = jnp.concatenate([none, g], 0)
        lane = lax.broadcasted_iota(jnp.int32, (1, wide), 1)
        q_place = jnp.where(lane < STRETCH, ra * STRETCH + lane, rb * STRETCH + lane - STRETCH)
        clear = ra // CHUNK
        total = (rb + CHUNK) // CHUNK

        def score(j, top, masked):
            s = jnp.dot(keys(j), q_low, preferred_element_type=f32)
            if masked:
                k_place = j * span + lax.broadcasted_iota(jnp.int32, (span, 1), 0)
                s = jnp.where(k_place <= q_place, s, BIG_NEG)
            probs[j] = s
            return jnp.maximum(top, jnp.max(s.reshape(span // 8, 8, wide), 0))

        top = jnp.full((8, wide), BIG_NEG, f32)
        top = lax.fori_loop(0, clear, lambda j, v: score(j, v, False), top)
        top = lax.fori_loop(clear, total, lambda j, v: score(j, v, True), top)
        top = jnp.max(top, 0, keepdims=True)

        def weigh(j, state):
            count, out = state
            weight = jnp.exp(probs[j] - top)
            probs[j] = weight
            count = count + jnp.sum(weight.reshape(span // 8, 8, wide), 0)
            out = out + jnp.dot(side(j, 1), weight.astype(bf16), preferred_element_type=f32)
            return count, out

        count, out = lax.fori_loop(
            0, total, weigh, (jnp.zeros((8, wide), f32), jnp.zeros((HEAD, wide), f32))
        )
        inverse = 1.0 / jnp.sum(count, 0, keepdims=True)
        out = out * inverse
        delta = jnp.sum(out * g.astype(f32), 0, keepdims=True)
        o_ref[:, at_a] = out[:, :STRETCH].astype(bf16)
        o_ref[:, at_b] = out[:, STRETCH:].astype(bf16)
        right = jnp.concatenate(
            [jnp.concatenate([g, none], 0).T, jnp.concatenate([none, q], 0).T], 0
        )

        def back(j, d_q):
            weight = probs[j] * inverse
            d_weight = jnp.dot(keys(j), g_high, preferred_element_type=f32)
            d_score = (weight * (d_weight - delta)).astype(bf16)
            left = jnp.concatenate([weight.astype(bf16), d_score], 1)
            sums[pl.ds(j * CHUNK, CHUNK)] += jnp.dot(
                left, right, preferred_element_type=f32
            ).reshape(CHUNK, STRETCH, 2 * HEAD)
            return d_q + jnp.dot(side(j, 0), d_score, preferred_element_type=f32)

        d_q = lax.fori_loop(0, total, back, jnp.zeros((HEAD, wide), f32))
        d_q = d_q * HEAD ** (-0.5)
        dq_ref[:, at_a] = d_q[:, :STRETCH]
        dq_ref[:, at_b] = d_q[:, STRETCH:]
        return carry

    lax.fori_loop(0, own // 2, pair, 0)
    for t in range(n_keys):
        i, at = t // own, (t % own) * STRETCH
        turned = sums[rank[t]].T.astype(bf16)
        dkv_ref[i, 1, :, at : at + STRETCH] = turned[:HEAD]
        dkv_ref[i, 0, :, at : at + STRETCH] = turned[HEAD:]


def attend(ranks, q, g, kv):
    heads, _, count = q.shape
    devices = kv.shape[0]
    n_keys = devices * count // STRETCH
    pairs = heads * 4 * HEAD * count * count * devices
    q_spec = pl.BlockSpec((None, HEAD, count), lambda h, *_: (h, 0, 0))
    kv_spec = pl.BlockSpec((devices, 2, None, HEAD, count), lambda h, *_: (0, 0, h, 0, 0))
    return pl.pallas_call(
        attend_kernel,
        grid_spec=pltpu.PrefetchScalarGridSpec(
            num_scalar_prefetch=1,
            grid=(heads,),
            in_specs=[q_spec, q_spec, kv_spec],
            out_specs=[q_spec, q_spec, kv_spec],
            scratch_shapes=[
                pltpu.VMEM((n_keys, STRETCH, 2 * HEAD), bf16),
                pltpu.VMEM((n_keys, 2 * HEAD, STRETCH), bf16),
                pltpu.VMEM((n_keys, STRETCH, 2 * HEAD), f32),
                pltpu.VMEM((n_keys // CHUNK, CHUNK * STRETCH, 2 * STRETCH), f32),
                pltpu.SMEM((count // STRETCH,), jnp.int32),
            ],
        ),
        out_shape=[
            jax.ShapeDtypeStruct(q.shape, bf16),
            jax.ShapeDtypeStruct(q.shape, f32),
            jax.ShapeDtypeStruct(kv.shape, bf16),
        ],
        compiler_params=pltpu.CompilerParams(vmem_limit_bytes=40 * 2**20),
        cost_estimate=pl.CostEstimate(
            flops=2 * pairs, bytes_accessed=4 * kv.size, transcendentals=pairs // 512
        ),
        name="attend",
    )(ranks, q, g, kv)


def angles_of(places):
    halfway = ROT // 2
    freqs = 10000.0 ** (-(jnp.arange(halfway, dtype=f32) * 2.0) / ROT)
    angles = freqs[:, None] * places.astype(f32)[None, :]
    return jnp.cos(angles), jnp.sin(angles)


def rotate(heads, cosine, sine):
    halfway = ROT // 2
    first = heads[:, :halfway]
    second = heads[:, halfway:ROT]
    return jnp.concatenate(
        [first * cosine - second * sine, second * cosine + first * sine, heads[:, ROT:]], 1
    )


def around(values):
    return [values] + [swap(values, "ulysses", j) for j in range(1, lax.axis_size("ulysses"))]


def mlp_pair(x, e, gain, shift, up_weight, up_bias, down_weight):
    side = lax.axis_index("fsdp")
    rows, width = x.shape
    units = up_weight.shape[1] // 2
    x_both = jnp.concatenate([x, swap(x, "fsdp", 1)], 0)
    e_both = jnp.concatenate([e, swap(e, "fsdp", 1)], 0)
    left, right = up_weight[:, :units], up_weight[:, units:]
    mine = jnp.where(side == 0, left, right)
    theirs = jnp.where(side == 0, right, left)
    up = in_order(side, mine, other_rows(theirs))
    normed = layer_norm(x_both.astype(f32), gain, shift).astype(bf16)
    hidden = jnp.dot(normed, up, preferred_element_type=f32) + up_bias.astype(f32)
    active_f, pull_gelu = jax.vjp(gelu_exact, hidden)
    active = active_f.astype(bf16)
    part = jnp.dot(active, down_weight, preferred_element_type=f32)
    out = part[:rows] + swap(part[rows:].astype(bf16), "fsdp", 1).astype(f32)
    d_active = jnp.einsum("td,fd->tf", e_both, down_weight, preferred_element_type=f32)
    d_hidden = pull_gelu(d_active)[0].astype(bf16)
    g_up_bias = jnp.sum(d_hidden.astype(f32), 0)
    d_part = jnp.einsum("tf,df->td", d_hidden, up, preferred_element_type=f32)
    d_normed = d_part[:rows] + swap(d_part[rows:].astype(bf16), "fsdp", 1).astype(f32)
    g_up = jnp.einsum(
        "td,tcf->cdf", normed, d_hidden.reshape(2 * rows, 2, units // 2), preferred_element_type=f32
    ).astype(bf16)
    g_down = jnp.einsum("tf,td->fd", active, e_both, preferred_element_type=f32).astype(bf16)
    g_down = g_down.reshape(2, units // 2, width)
    pieces = jnp.stack([g_up, g_down], 1).reshape(2, 2, 2, width // 2, width)
    sums = add_half((pieces[0], pieces[1]), "blk", 1)
    sums = add_half(halves_of(sums, 2), "blk", 2)
    sums = add_half(halves_of(sums, 2), "ulysses", 1)
    sums = add_half(halves_of(sums, 2), "ulysses", 2)
    got = swap(jnp.where(side == 0, sums[0, 1], sums[0, 0]), "fsdp", 1)
    kept = jnp.where(side == 0, sums[0, 0], sums[0, 1])
    sums = jnp.concatenate([in_order(side, kept[None], got[None]), sums[1]], 0)
    sums = share_half(sums, "ulysses", 2, 1)
    sums = share_half(sums, "ulysses", 1, 1)
    sums = share_half(sums, "blk", 2, 1)
    sums = share_half(sums[None], "blk", 1, 0).astype(f32)
    g_up = jnp.concatenate([sums[c, f] for f in range(2) for c in range(2)], 1)
    g_down = sums[:, 2:].reshape(2 * width, width)
    full_bias = jnp.where(side == 0, jnp.concatenate([g_up_bias, 0 * g_up_bias]), jnp.concatenate([0 * g_up_bias, g_up_bias]))
    return out, d_normed, g_up, g_down, full_bias


def mlp_gathered(x, e, gain, shift, up_weight, up_bias, down_weight):
    up, down = gather_rows(up_weight), gather_rows(down_weight)
    bias = gather_small(up_bias).reshape(-1)
    normed = layer_norm(x.astype(f32), gain, shift).astype(bf16)
    hidden = jnp.dot(normed, up, preferred_element_type=f32) + bias.astype(f32)
    active_f, pull_gelu = jax.vjp(gelu_exact, hidden)
    active = active_f.astype(bf16)
    out = jnp.dot(active, down, preferred_element_type=f32)
    g_down = jnp.einsum("tf,td->fd", active, e, preferred_element_type=f32)
    d_active = jnp.einsum("td,fd->tf", e, down, preferred_element_type=f32)
    d_hidden = pull_gelu(d_active)[0].astype(bf16)
    g_up = jnp.einsum("td,tf->df", normed, d_hidden, preferred_element_type=f32)
    d_normed = jnp.einsum("tf,df->td", d_hidden, up, preferred_element_type=f32)
    g_up, g_down = (
        lax.psum(
            lax.psum_scatter(g.astype(bf16), "fsdp", scatter_dimension=0, tiled=True),
            ("blk", "ulysses"),
        ).astype(f32)
        for g in (g_up, g_down)
    )
    return out, d_normed, g_up, g_down, jnp.sum(d_hidden.astype(f32), 0)


def attention_grads(grads):
    _, cols, width = grads.shape
    groups = lax.axis_size("ulysses")
    if lax.axis_size("fsdp") != 2:
        shards = lax.axis_size("fsdp")
        total = lax.psum(grads, ("blk", "fsdp"))
        total = lax.all_gather(total, "ulysses", axis=1, tiled=True)
        rows = width // shards
        first = lax.axis_index("fsdp") * rows
        g_qkv = lax.dynamic_slice_in_dim(total[:3], first, rows, 2)
        g_out = lax.dynamic_slice_in_dim(total[3], first, rows, 0)
        return g_qkv.reshape(3 * width, rows).T.astype(f32), g_out.astype(f32)
    side = lax.axis_index("fsdp")
    group = lax.axis_index("ulysses")
    half = width // 2
    grads = add_half(halves_of(grads, 1), "blk", 1)
    grads = add_half(halves_of(grads, 1), "blk", 2)
    rows = grads.shape[1]
    low, high = grads[:, :, :half], grads[:, :, half:]
    kept = jnp.where(side == 0, low[:3], high[:3])
    sent = jnp.where(side == 0, high[:3], low[:3])
    whole = jnp.stack([low[3], high[3]])
    kept = jnp.concatenate([kept, whole])
    got = swap(jnp.concatenate([sent, whole]), "fsdp", 1)
    kept = (kept.astype(f32) + got.astype(f32)).astype(bf16)[None]
    for bit in (1, 2):
        kept = share_half(kept, "ulysses", bit, 0)
    of_qkv = kept[:, :3].reshape(3 * groups, rows, half)
    of_out = jnp.where(side == 0, kept[: groups // 2, 3:], kept[groups // 2 :, 3:])
    kept = jnp.concatenate([of_qkv, of_out.reshape(groups, rows, half)])
    kept = share_half(kept, "blk", 2, 1)
    kept = share_half(kept, "blk", 1, 1)
    g_qkv = kept[: 3 * groups].reshape(groups, 3, cols, half).transpose(3, 1, 0, 2)
    g_out = kept[3 * groups :].reshape(groups // 2, 2, cols, half).transpose(0, 2, 1, 3)
    return g_qkv.reshape(half, 3 * width).astype(f32), g_out.reshape(half, width).astype(f32)


def sum_everywhere(values):
    for axis in ("blk", "ulysses", "fsdp"):
        step = 1
        while step < lax.axis_size(axis):
            values = values + swap(values, axis, step)
            step *= 2
    return values


def on_device(
    tokens,
    positions,
    cotangent,
    ln1_gain,
    ln1_bias,
    ln2_gain,
    ln2_bias,
    qkv_weight,
    qkv_bias,
    out_weight,
    out_bias,
    up_weight,
    up_bias,
    down_weight,
    down_bias,
):
    count, width = tokens.shape
    groups = lax.axis_size("ulysses")
    group = lax.axis_index("ulysses")
    shards = lax.axis_size("fsdp")
    cols = width // groups
    heads = cols // HEAD
    rows = count * groups

    x_all = jnp.concatenate(around(tokens), 0)
    w_qkv = gather_rows(qkv_weight)
    small = gather_small(
        jnp.concatenate([ln1_gain, ln1_bias, ln2_gain, ln2_bias, out_bias, down_bias, qkv_bias])
    )
    part = width // shards
    ln1_g, ln1_b, ln2_g, ln2_b, b_out, b_down = (
        small[:, i * part : (i + 1) * part].reshape(width).astype(f32) for i in range(6)
    )
    b_qkv = small[:, 6 * part :].reshape(3 * width).astype(f32)
    ranks = positions[::STRETCH] // STRETCH
    for axis in ("ulysses", "blk"):
        step = 1
        while step < lax.axis_size(axis):
            ranks = jnp.concatenate([ranks, swap(ranks, axis, step)])
            step *= 2
    places = (ranks[: rows // STRETCH, None] * STRETCH + jnp.arange(STRETCH)[None, :]).reshape(-1)
    cosine, sine = angles_of(places)
    e_all = jnp.concatenate(around(cotangent), 0)

    if shards == 2:
        mlp = mlp_pair
    else:
        mlp = mlp_gathered
    mlp_out, d_norm_two, g_up, g_down, g_up_bias = mlp(
        tokens, cotangent, ln2_g, ln2_b, up_weight, up_bias, down_weight
    )

    normed = layer_norm(x_all.astype(f32), ln1_g, ln1_b).astype(bf16)
    starts = [i * width + group * cols for i in range(3)]
    w_mine = jnp.concatenate([lax.dynamic_slice_in_dim(w_qkv, s, cols, 1) for s in starts], 1)
    b_mine = jnp.concatenate([lax.dynamic_slice_in_dim(b_qkv, s, cols, 0) for s in starts])
    joined = jnp.einsum("de,td->et", w_mine, normed, preferred_element_type=f32) + b_mine[:, None]
    joined = joined.reshape(3, heads, HEAD, rows)
    queries = (rotate(joined[0], cosine, sine).astype(bf16) * HEAD ** (-0.5)).astype(bf16)
    kv = jnp.stack([rotate(joined[1], cosine, sine).astype(bf16), joined[2].astype(bf16)])
    pieces = {0: kv}
    step = lax.axis_size("blk") // 2
    while step >= 1:
        for i in list(pieces):
            pieces[i ^ step] = swap(pieces[i], "blk", step)
        step //= 2
    kv_all = jnp.stack([pieces[i] for i in range(len(pieces))])

    w_out = gather_rows(out_weight)
    w_out_mine = lax.dynamic_slice_in_dim(w_out, group * cols, cols, 0)
    d_heads = jnp.einsum("ed,td->et", w_out_mine, e_all, preferred_element_type=f32).astype(bf16)
    mixed, d_q, d_kv = attend(ranks, queries, d_heads.reshape(heads, HEAD, rows), kv_all)

    mixed = mixed.reshape(cols, rows)
    back = [mixed[:, j * count : (j + 1) * count] for j in range(groups)]
    back = [back[0]] + [swap(back[j], "ulysses", j) for j in range(1, groups)]
    mixed_mine = jnp.concatenate(by_device(back, group), 0)
    attn_out = jnp.einsum("et,ed->td", mixed_mine, w_out, preferred_element_type=f32)
    x_float = tokens.astype(f32)
    output = (x_float + (attn_out + b_out) + (mlp_out + b_down)).astype(bf16)

    blks = lax.axis_size("blk")
    d_kv = [d_kv[i] for i in range(blks)]
    step = 1
    while step < blks:
        sent = [swap(d_kv[i], "blk", step) for i in range(step, blks, 2 * step)]
        kept = [d_kv[i] for i in range(0, blks, 2 * step)]
        total = [a.astype(f32) + b.astype(f32) for a, b in zip(kept, sent)]
        step *= 2
        if step < blks:
            total = [a.astype(bf16) for a in total]
        d_kv = [total[i // step] if i % step == 0 else None for i in range(blks)]
    d_kv = d_kv[0]
    d_joined = jnp.concatenate(
        [
            rotate(d_q, cosine, -sine).astype(bf16),
            rotate(d_kv[0], cosine, -sine).astype(bf16),
            d_kv[1].astype(bf16),
        ],
        0,
    ).reshape(3 * cols, rows)
    g_bias_mine = jnp.sum(d_joined.astype(f32), 1)
    g_qkv = jnp.dot(d_joined, normed, preferred_element_type=f32).astype(bf16)
    g_out = jnp.dot(mixed, e_all, preferred_element_type=f32).astype(bf16)
    g_qkv, g_out = attention_grads(
        jnp.concatenate([g_qkv.reshape(3, cols, width), g_out[None]])
    )

    back = [d_joined[:, j * count : (j + 1) * count] for j in range(groups)]
    back = [back[0]] + [swap(back[j], "ulysses", j) for j in range(1, groups)]
    back = by_device(back, group)
    d_mine = jnp.concatenate([back[z][i * cols : (i + 1) * cols] for i in range(3) for z in range(groups)], 0)
    d_norm_one = jnp.einsum("et,de->td", d_mine, w_qkv, preferred_element_type=f32)
    _, pull_one = jax.vjp(layer_norm, x_float, ln1_g, ln1_b)
    _, pull_two = jax.vjp(layer_norm, x_float, ln2_g, ln2_b)
    d_x_one, g_ln1_g, g_ln1_b = pull_one(d_norm_one)
    d_x_two, g_ln2_g, g_ln2_b = pull_two(d_norm_two)
    e_float = cotangent.astype(f32)
    input_grad = (e_float + d_x_one + d_x_two).astype(bf16)

    g_qkv_bias = jnp.zeros((3, groups, cols), f32)
    g_qkv_bias = lax.dynamic_update_slice(g_qkv_bias, g_bias_mine.reshape(3, 1, cols), (0, group, 0))
    vectors = [g_ln1_g, g_ln1_b, g_ln2_g, g_ln2_b, jnp.sum(e_float, 0), g_qkv_bias.reshape(-1), g_up_bias]
    summed = sum_everywhere(jnp.concatenate(vectors))
    results, start = [], 0
    for vector in vectors:
        mine = vector.shape[0] // shards
        results.append(lax.dynamic_slice_in_dim(summed, start + lax.axis_index("fsdp") * mine, mine))
        start += vector.shape[0]
    g_ln1_g, g_ln1_b, g_ln2_g, g_ln2_b, g_e, g_qkv_bias, g_up_bias = results
    return (
        output,
        input_grad,
        g_ln1_g,
        g_ln1_b,
        g_ln2_g,
        g_ln2_b,
        g_qkv,
        g_qkv_bias,
        g_out,
        g_e,
        g_up,
        g_up_bias,
        g_down,
        g_e,
    )


def solution(mesh):
    rows = P(("fsdp", "blk", "ulysses"), None)
    split, matrix = P("fsdp"), P("fsdp", None)
    return jax.shard_map(
        on_device,
        mesh=mesh,
        in_specs=(
            rows,
            P(("fsdp", "blk", "ulysses")),
            rows,
            split,
            split,
            split,
            split,
            matrix,
            split,
            matrix,
            split,
            matrix,
            split,
            matrix,
            split,
        ),
        out_specs=(
            rows,
            rows,
            split,
            split,
            split,
            split,
            matrix,
            split,
            matrix,
            split,
            matrix,
            split,
            matrix,
            split,
        ),
        check_vma=False,
    )
```

time: 834 us -> 534 us (0.64); the launches traced: 825 us -> 536 us
  blocking collectives: 174 us -> 0 us
  matrix products: 187 us -> 31.5 us
  Pallas kernels: 0 us -> 102 us
  starting transfers between devices: 21.1 us -> 81.1 us
  waiting for transfers between devices: 275 us -> 216 us
  local copies, waits for them, and re-layouts: 81.4 us -> 48.2 us
  between operations: 17.1 us -> 2.37 us
  other arithmetic: 66.8 us -> 54.9 us
    ppermute x0 -> x57, waiting for transfers between devices: none -> 216 us  [swap(): return lax.ppermute(values, axis, [(i, i ^ bits) for i in range(count)])]
    reduce_scatter x6 -> x0, waiting for transfers between devices: 169 us -> none  [the longest x4 168 us: on_device(): lax.psum_scatter(shortened(attn_grads + mlp_grads), 'fsdp', scatter_dimen...]
    dot_general x68 -> x12, matrix products: 187 us -> 31.5 us  [the longest x1 9.33 us: mlp_pair(): jnp.einsum('td,fd->tf', e_both, down_weight, preferred_element_type=f32)]
    pallas_call x0 -> x1, Pallas kernels: none -> 102 us  [attend(): pl.pallas_call(attend_kernel, grid_spec=pltpu.PrefetchScalarGridSpec(num_...]
    ppermute x0 -> x57, starting transfers between devices: none -> 81.1 us  [swap(): return lax.ppermute(values, axis, [(i, i ^ bits) for i in range(count)])]
    psum x1 -> x0, waiting for transfers between devices: 59.9 us -> none  [on_device(): lax.psum(shortened(shards), ('blk', 'ulysses'))]
    psum x1 -> x0, blocking collectives: 59.2 us -> none  [on_device(): lax.psum(shortened(shards), ('blk', 'ulysses'))]
    all_gather x9 -> x0, blocking collectives: 55.7 us -> none  [the longest x1 30.2 us: on_device(): lax.all_gather(positions, ('blk', 'ulysses'), axis=0, tiled=True)]
  transfers between devices with their start and end apart: 17 -> 57, of which waited for: 8 -> 24; matrix products, arithmetic and copies ran while one was open for 37% -> 22% of each run, Pallas kernels for 0% -> 19%
where the time goes in v1:
time: 534 us; the launch traced here: 536 us
  waiting for transfers between devices  216 us (40%)
  Pallas kernels  102 us (19%)
  starting transfers between devices  81.1 us (15%)
  other arithmetic  54.9 us (10%)
  local copies, waits for them, and re-layouts  48.2 us (9%)
  matrix products  31.5 us (6%)
    ppermute x57, waiting for transfers between devices, swap(): return lax.ppermute(values, axis, [(i, i ^ bits) for i in range(count)])  216 us
    pallas_call x1, Pallas kernels, attend(): pl.pallas_call(attend_kernel, grid_spec=pltpu.PrefetchScalarGridSpec(num_...  102 us
    ppermute x57, starting transfers between devices, swap(): return lax.ppermute(values, axis, [(i, i ^ bits) for i in range(count)])  81.1 us
    unnamed x181, local copies, waits for them, and re-layouts  23.2 us
  transfers between devices with their start and end apart: 57, of which 24 were waited for; matrix products, arithmetic and copies ran while one was open for 22% of the time, Pallas kernels for 19%

profile of v1, /device:TPU:9, one launch (start us, length us, event | category | flops | bytes accessed | tf_op | source)
XLA Modules:
  0.0 535.8 jit_solution(17723414400796290204)
XLA Ops:
  22.9 3.2 fusion.96
  29.4 22.9 %collective-permute-done.1 = s32[4]{0:T(128)S(1)} collective-permute-done((s32[4]{0:T(128)S(1)}, s32[4]{0:T(128)S(1)}, u32[]{:S(2)}, u32[]{:S(2)}) %collective-permute-start.1) | collective-permute-done | bytes 48 | tf_op jit(solution)/shard_map/ppermute | solution.py:31
  83.1 21.8 %collective-permute-done.24 = bf16[96,1536]{1,0:T(8,128)(2,1)S(1)} collective-permute-done((bf16[96,1536]{1,0:T(8,128)(2,1)S(1)}, bf16[96,1536]{1,0:T(8,128)(2,1)S(1)}, u32[]{:S(2)}, u32[]{:S(2)}) %collective-permute-start.24) | collective-permute-done | bytes 294944 | tf_op jit(solution)/shard_map/ppermute | solution.py:31
  106.0 3.4 collective-permute-start.13
  111.6 7.6 %collective-permute-done.5 = bf16[96,2304]{1,0:T(8,128)(2,1)S(1)} collective-permute-done((bf16[96,2304]{1,0:T(8,128)(2,1)S(1)}, bf16[96,2304]{1,0:T(8,128)(2,1)S(1)}, u32[]{:S(2)}, u32[]{:S(2)}) %collective-permute-start.5) | collective-permute-done | bytes 442400 | tf_op jit(solution)/shard_map/ppermute | solution.py:31
  119.2 5.5 %collective-permute-start.26 = (bf16[192,1536]{1,0:T(8,128)(2,1)S(1)}, bf16[192,1536]{1,0:T(8,128)(2,1)S(1)}, u32[]{:S(2)}, u32[]{:S(2)}) collective-permute-start(bf16[192,1536]{1,0:T(8,128)(2,1)S(1)} %pad_maximum_fusion.23), channel_id=1, source_target_pairs={{0,4},{4,0},{8,12},{12,8},{1,5},{5,1},{9,13},{13,9},{2,6},{6,2},{1... | collective-permute-start | bytes 1769480 | tf_op jit(solution)/shard_map/ppermute | solution.py:31
  130.3 9.3 %convert_reduce_fusion.1 = (f32[1536]{0:T(1024)}, bf16[512,1536]{1,0:T(8,128)(2,1)S(1)}, f32[512,1536]{1,0:T(8,128)S(1)}) fusion(f32[512,1536]{1,0:T(8,128)S(1)} %convolution_add_fusion, bf16[512,768]{1,0:T(8,128)(2,1)S(1)} %constant_dynamic-update-slice_fusion.4, bf16[1536,768]{1,0:T(8,128)(2,1)S(1)} %copy-done), kind=kOutput, calls=%fused_computation.27 | convolution fusion | flops 1266153984 | bytes 11016192 | tf_op jit(solution)/shard_map/td,fd->tf/dot_general | solution.py:261
  147.5 3.0 convolution_add_fusion.1
  155.1 15.4 %collective-permute-done.18 = bf16[2,3,64,1024]{3,2,1,0:T(8,128)(2,1)S(1)} collective-permute-done((bf16[2,3,64,1024]{3,2,1,0:T(8,128)(2,1)S(1)}, bf16[2,3,64,1024]{3,2,1,0:T(8,128)(2,1)S(1)}, u32[]{:S(2)}, u32[]{:S(2)}) %collective-permute-start.18) | collective-permute-done | bytes 786464 | tf_op jit(solution)/shard_map/ppermute | solution.py:31
  173.8 101.8 %attend.1 = (bf16[3,64,1024]{2,1,0:T(8,128)(2,1)S(1)}, f32[3,64,1024]{2,1,0:T(8,128)S(1)}, bf16[4,2,3,64,1024]{4,3,2,1,0:T(8,128)(2,1)S(1)}) custom-call(s32[32]{0:T(128)S(1)} %concatenate.164.rank, bf16[3,64,1024]{2,1,0:T(8,128)(2,1)S(1)} %maximum_multiply_fusion.q_ref, bf16[3,64,1024]{2,1,0:T(8,128)(2,1)S(1)} %bitcast.112, ...), custom_call_target="tpu_custom_call" | custom-call | flops 6442450944 | bytes 6291456 | tf_op jit(solution)/shard_map/attend/pallas_call | solution.py:197
  279.6 18.8 %collective-permute-start.49 = (bf16[2,2,192,768]{3,2,1,0:T(8,128)(2,1)}, bf16[2,2,192,768]{3,2,1,0:T(8,128)(2,1)}, u32[]{:S(2)}, u32[]{:S(2)}) collective-permute-start(bf16[2,2,192,768]{3,2,1,0:T(8,128)(2,1)} %broadcast_select_fusion.6), channel_id=1, source_target_pairs={{0,8},{4,12},{8,0},{12,4},{1,9},{5,13},{9,1},{13,5},{2,10},{6,14},... | collective-permute-start | bytes 3538952 | tf_op jit(solution)/shard_map/ppermute | solution.py:31
  298.5 3.7 fusion.27
  307.4 17.5 %collective-permute-done.49 = bf16[2,2,192,768]{3,2,1,0:T(8,128)(2,1)} collective-permute-done((bf16[2,2,192,768]{3,2,1,0:T(8,128)(2,1)}, bf16[2,2,192,768]{3,2,1,0:T(8,128)(2,1)}, u32[]{:S(2)}, u32[]{:S(2)}) %collective-permute-start.49) | collective-permute-done | bytes 1179680 | tf_op jit(solution)/shard_map/ppermute | solution.py:31
  329.2 12.7 %collective-permute-done.30 = bf16[2,3,64,1024]{3,2,1,0:T(8,128)(2,1)S(1)} collective-permute-done((bf16[2,3,64,1024]{3,2,1,0:T(8,128)(2,1)S(1)}, bf16[2,3,64,1024]{3,2,1,0:T(8,128)(2,1)S(1)}, u32[]{:S(2)}, u32[]{:S(2)}) %collective-permute-start.30) | collective-permute-done | bytes 786464 | tf_op jit(solution)/shard_map/ppermute | solution.py:31
  347.2 3.4 convolution_convert_fusion.1
  352.1 5.4 %collective-permute-done.33 = bf16[576,256]{1,0:T(8,128)(2,1)} collective-permute-done((bf16[576,256]{1,0:T(8,128)(2,1)}, bf16[576,256]{1,0:T(8,128)(2,1)}, u32[]{:S(2)}, u32[]{:S(2)}) %collective-permute-start.33) | collective-permute-done | bytes 294944 | tf_op jit(solution)/shard_map/ppermute | solution.py:31
  360.1 12.7 %collective-permute-done.31 = bf16[576,256]{1,0:T(8,128)(2,1)} collective-permute-done((bf16[576,256]{1,0:T(8,128)(2,1)}, bf16[576,256]{1,0:T(8,128)(2,1)}, u32[]{:S(2)}, u32[]{:S(2)}) %collective-permute-start.31) | collective-permute-done | bytes 294944 | tf_op jit(solution)/shard_map/ppermute | solution.py:31
  382.9 10.1 %collective-permute-done.51 = bf16[2,2,48,768]{3,2,1,0:T(8,128)(2,1)S(1)} collective-permute-done((bf16[2,2,48,768]{3,2,1,0:T(8,128)(2,1)S(1)}, bf16[2,2,48,768]{3,2,1,0:T(8,128)(2,1)S(1)}, u32[]{:S(2)}, u32[]{:S(2)}) %collective-permute-start.51) | collective-permute-done | bytes 294944 | tf_op jit(solution)/shard_map/ppermute | solution.py:31
  395.0 3.4 collective-permute-done.43
  398.4 4.3 collective-permute-start.44
  402.8 4.4 collective-permute-done.44
  407.4 14.4 %collective-permute-done.53 = bf16[4,48,768]{2,1,0:T(8,128)(2,1)S(1)} collective-permute-done((bf16[4,48,768]{2,1,0:T(8,128)(2,1)S(1)}, bf16[4,48,768]{2,1,0:T(8,128)(2,1)S(1)}, u32[]{:S(2)}, u32[]{:S(2)}) %collective-permute-start.53) | collective-permute-done | bytes 294944 | tf_op jit(solution)/shard_map/ppermute | solution.py:31
  421.9 3.2 collective-permute-start.54
  425.0 4.8 collective-permute-done.45
  430.0 15.2 %collective-permute-done.54 = bf16[4,96,768]{2,1,0:T(8,128)(2,1)S(1)} collective-permute-done((bf16[4,96,768]{2,1,0:T(8,128)(2,1)S(1)}, bf16[4,96,768]{2,1,0:T(8,128)(2,1)S(1)}, u32[]{:S(2)}, u32[]{:S(2)}) %collective-permute-start.54) | collective-permute-done | bytes 589856 | tf_op jit(solution)/shard_map/ppermute | solution.py:31
  452.3 33.1 %collective-permute-done.46 = bf16[16,48,384]{2,1,0:T(8,128)(2,1)S(1)} collective-permute-done((bf16[16,48,384]{2,1,0:T(8,128)(2,1)S(1)}, bf16[16,48,384]{2,1,0:T(8,128)(2,1)S(1)}, u32[]{:S(2)}, u32[]{:S(2)}) %collective-permute-start.46) | collective-permute-done | bytes 589856 | tf_op jit(solution)/shard_map/ppermute | solution.py:31
  502.3 2.6 collective-permute-start.39
  504.9 3.4 collective-permute-done.20
  509.8 3.0 fusion.30
  521.4 5.2 copy.39
  526.6 2.8 broadcast_select_fusion.3
  532.3 2.8 pad_maximum_fusion.1
  (422 shorter events, 152.5 us)
Async XLA Ops:
  0.7 73.4 %collective-permute-start.9 = (bf16[256,768]{1,0:T(8,128)(2,1)}, bf16[256,768]{1,0:T(8,128)(2,1)S(1)}, u32[]{:S(2)}, u32[]{:S(2)}) collective-permute-start(bf16[256,768]{1,0:T(8,128)(2,1)} %param.15), channel_id=1, source_target_pairs={{0,3},{1,2},{2,1},{3,0},{4,7},{5,6},{6,5},{7,4},{8,11},{9,10},{10,... | collective-permute-start | bytes 1179656 | tf_op jit(solution)/shard_map/ppermute | solution.py:31
  2.0 73.1 %collective-permute-start.8 = (bf16[256,768]{1,0:T(8,128)(2,1)}, bf16[256,768]{1,0:T(8,128)(2,1)}, u32[]{:S(2)}, u32[]{:S(2)}) collective-permute-start(bf16[256,768]{1,0:T(8,128)(2,1)} %param.15), channel_id=1, source_target_pairs={{0,2},{1,3},{2,0},{3,1},{4,6},{5,7},{6,4},{7,5},{8,10},{9,11},{10,... | collective-permute-start | bytes 1179656 | tf_op jit(solution)/shard_map/ppermute | solution.py:31
  3.9 24.2 %collective-permute-start = (s32[2]{0:T(128)S(1)}, s32[2]{0:T(128)S(1)}, u32[]{:S(2)}, u32[]{:S(2)}) collective-permute-start(s32[2]{0:T(128)S(1)} %and_select_fusion), channel_id=1, source_target_pairs={{0,1},{1,0},{2,3},{3,2},{4,5},{5,4},{6,7},{7,6},{8,9},{9,8},{10,11... | collective-permute-start | bytes 32 | tf_op jit(solution)/shard_map/ppermute | solution.py:31
  11.7 49.8 %collective-permute-start.10 = (bf16[1,3456]{1,0:T(2,128)(2,1)}, bf16[1,3456]{1,0:T(2,128)(2,1)}, u32[]{:S(2)}, u32[]{:S(2)}) collective-permute-start(bf16[1,3456]{1,0:T(2,128)(2,1)} %broadcast_in_dim.18), channel_id=1, source_target_pairs={{0,16},{16,0},{1,17},{17,1},{2,18},{18,2},{3,19},{19,3},{4,20},{20... | collective-permute-start | bytes 20744 | tf_op jit(solution)/shard_map/ppermute | solution.py:31
  12.9 140.7 %collective-permute-start.16 = (bf16[256,768]{1,0:T(8,128)(2,1)}, bf16[256,768]{1,0:T(8,128)(2,1)}, u32[]{:S(2)}, u32[]{:S(2)}) collective-permute-start(bf16[256,768]{1,0:T(8,128)(2,1)} %param.17), channel_id=1, source_target_pairs={{0,3},{1,2},{2,1},{3,0},{4,7},{5,6},{6,5},{7,4},{8,11},{9,10},{10,... | collective-permute-start | bytes 1179656 | tf_op jit(solution)/shard_map/ppermute | solution.py:31
  28.1 24.1 %collective-permute-start.1 = (s32[4]{0:T(128)S(1)}, s32[4]{0:T(128)S(1)}, u32[]{:S(2)}, u32[]{:S(2)}) collective-permute-start(s32[4]{0:T(128)S(1)} %pad_add_fusion), channel_id=1, source_target_pairs={{0,2},{1,3},{2,0},{3,1},{4,6},{5,7},{6,4},{7,5},{8,10},{9,11},{10,... | collective-permute-start | bytes 56 | tf_op jit(solution)/shard_map/ppermute | solution.py:31
  74.1 79.4 %collective-permute-start.15 = (bf16[256,768]{1,0:T(8,128)(2,1)S(1)}, bf16[256,768]{1,0:T(8,128)(2,1)S(1)}, u32[]{:S(2)}, u32[]{:S(2)}) collective-permute-start(bf16[256,768]{1,0:T(8,128)(2,1)S(1)} %copy-done.32), channel_id=1, source_target_pairs={{0,2},{1,3},{2,0},{3,1},{4,6},{5,7},{6,4},{7,5},{8,10},{9,11},{10,... | collective-permute-start | bytes 1179656 | tf_op jit(solution)/shard_map/ppermute | solution.py:31
  75.2 30.0 %collective-permute-start.34 = (bf16[256,768]{1,0:T(8,128)(2,1)S(1)}, bf16[256,768]{1,0:T(8,128)(2,1)S(1)}, u32[]{:S(2)}, u32[]{:S(2)}) collective-permute-start(bf16[256,768]{1,0:T(8,128)(2,1)S(1)} %copy-done.32), channel_id=1, source_target_pairs={{0,16},{16,0},{1,17},{17,1},{2,18},{18,2},{3,19},{19,3},{4,20},{20... | collective-permute-start | bytes 1179656 | tf_op jit(solution)/shard_map/ppermute | solution.py:31
  75.9 30.0 %collective-permute-start.4 = (bf16[96,2304]{1,0:T(8,128)(2,1)}, bf16[96,2304]{1,0:T(8,128)(2,1)S(1)}, u32[]{:S(2)}, u32[]{:S(2)}) collective-permute-start(bf16[96,2304]{1,0:T(8,128)(2,1)} %constant_dynamic-slice_fusion.1), channel_id=1, source_target_pairs={{0,16},{16,0},{1,17},{17,1},{2,18},{18,2},{3,19},{19,3},{4,20},{20... | collective-permute-start | bytes 1327112 | tf_op jit(solution)/shard_map/ppermute | solution.py:31
  80.6 24.2 %collective-permute-start.24 = (bf16[96,1536]{1,0:T(8,128)(2,1)S(1)}, bf16[96,1536]{1,0:T(8,128)(2,1)S(1)}, u32[]{:S(2)}, u32[]{:S(2)}) collective-permute-start(bf16[96,1536]{1,0:T(8,128)(2,1)S(1)} %copy-done.44), channel_id=1, source_target_pairs={{0,16},{16,0},{1,17},{17,1},{2,18},{18,2},{3,19},{19,3},{4,20},{20... | collective-permute-start | bytes 884744 | tf_op jit(solution)/shard_map/ppermute | solution.py:31
  104.8 47.7 %collective-permute-start.14 = (bf16[256,768]{1,0:T(8,128)(2,1)S(1)}, bf16[256,768]{1,0:T(8,128)(2,1)S(1)}, u32[]{:S(2)}, u32[]{:S(2)}) collective-permute-start(bf16[256,768]{1,0:T(8,128)(2,1)S(1)} %copy-done.32), channel_id=1, source_target_pairs={{0,1},{1,0},{2,3},{3,2},{4,5},{5,4},{6,7},{7,6},{8,9},{9,8},{10,11... | collective-permute-start | bytes 1179656 | tf_op jit(solution)/shard_map/ppermute | solution.py:31
  106.0 65.5 %collective-permute-start.13 = (bf16[192,768]{1,0:T(8,128)(2,1)S(1)}, bf16[192,768]{1,0:T(8,128)(2,1)S(1)}, u32[]{:S(2)}, u32[]{:S(2)}) collective-permute-start(bf16[192,768]{1,0:T(8,128)(2,1)S(1)} %pad_maximum_fusion.28), channel_id=1, source_target_pairs={{0,4},{4,0},{8,12},{12,8},{1,5},{5,1},{9,13},{13,9},{2,6},{6,2},{1... | collective-permute-start | bytes 884744 | tf_op jit(solution)/shard_map/ppermute | solution.py:31
  151.5 19.1 %collective-permute-start.18 = (bf16[2,3,64,1024]{3,2,1,0:T(8,128)(2,1)S(1)}, bf16[2,3,64,1024]{3,2,1,0:T(8,128)(2,1)S(1)}, u32[]{:S(2)}, u32[]{:S(2)}) collective-permute-start(bf16[2,3,64,1024]{3,2,1,0:T(8,128)(2,1)S(1)} %get-tuple-element.122), channel_id=1, source_target_pairs={{0,8},{4,12},{8,0},{12,4},{1,9},{5,13},{9,1},{13,5},{2,10},{6,14},... | collective-permute-start | bytes 2359304 | tf_op jit(solution)/shard_map/ppermute | solution.py:31
  152.6 124.5 %collective-permute-start.48 = (bf16[2,2,384,768]{3,2,1,0:T(8,128)(2,1)S(1)}, bf16[2,2,384,768]{3,2,1,0:T(8,128)(2,1)S(1)}, u32[]{:S(2)}, u32[]{:S(2)}) collective-permute-start(bf16[2,2,384,768]{3,2,1,0:T(8,128)(2,1)S(1)} %bitcast.126), channel_id=1, source_target_pairs={{0,4},{4,0},{8,12},{12,8},{1,5},{5,1},{9,13},{13,9},{2,6},{6,2},{1... | collective-permute-start | bytes 7077896 | tf_op jit(solution)/shard_map/ppermute | solution.py:31
  154.6 18.3 %collective-permute-start.17 = (bf16[2,3,64,1024]{3,2,1,0:T(8,128)(2,1)S(1)}, bf16[2,3,64,1024]{3,2,1,0:T(8,128)(2,1)S(1)}, u32[]{:S(2)}, u32[]{:S(2)}) collective-permute-start(bf16[2,3,64,1024]{3,2,1,0:T(8,128)(2,1)S(1)} %get-tuple-element.122), channel_id=1, source_target_pairs={{0,4},{4,0},{8,12},{12,8},{1,5},{5,1},{9,13},{13,9},{2,6},{6,2},{1... | collective-permute-start | bytes 2359304 | tf_op jit(solution)/shard_map/ppermute | solution.py:31
  277.0 25.7 %collective-permute-start.29 = (bf16[2,3,64,1024]{3,2,1,0:T(8,128)(2,1)}, bf16[2,3,64,1024]{3,2,1,0:T(8,128)(2,1)}, u32[]{:S(2)}, u32[]{:S(2)}) collective-permute-start(bf16[2,3,64,1024]{3,2,1,0:T(8,128)(2,1)} %get-tuple-element.85), channel_id=1, source_target_pairs={{0,4},{4,0},{8,12},{12,8},{1,5},{5,1},{9,13},{13,9},{2,6},{6,2},{1... | collective-permute-start | bytes 2359304 | tf_op jit(solution)/shard_map/ppermute | solution.py:31
  279.6 45.4 %collective-permute-start.49 = (bf16[2,2,192,768]{3,2,1,0:T(8,128)(2,1)}, bf16[2,2,192,768]{3,2,1,0:T(8,128)(2,1)}, u32[]{:S(2)}, u32[]{:S(2)}) collective-permute-start(bf16[2,2,192,768]{3,2,1,0:T(8,128)(2,1)} %broadcast_select_fusion.6), channel_id=1, source_target_pairs={{0,8},{4,12},{8,0},{12,4},{1,9},{5,13},{9,1},{13,5},{2,10},{6,14},... | collective-permute-start | bytes 3538952 | tf_op jit(solution)/shard_map/ppermute | solution.py:31
  302.2 27.0 %collective-permute-start.28 = (bf16[2,3,64,1024]{3,2,1,0:T(8,128)(2,1)S(1)}, bf16[2,3,64,1024]{3,2,1,0:T(8,128)(2,1)S(1)}, u32[]{:S(2)}, u32[]{:S(2)}) collective-permute-start(bf16[2,3,64,1024]{3,2,1,0:T(8,128)(2,1)S(1)} %copy-done.41), channel_id=1, source_target_pairs={{0,4},{4,0},{8,12},{12,8},{1,5},{5,1},{9,13},{13,9},{2,6},{6,2},{1... | collective-permute-start | bytes 2359304 | tf_op jit(solution)/shard_map/ppermute | solution.py:31
  304.7 37.2 %collective-permute-start.30 = (bf16[2,3,64,1024]{3,2,1,0:T(8,128)(2,1)S(1)}, bf16[2,3,64,1024]{3,2,1,0:T(8,128)(2,1)S(1)}, u32[]{:S(2)}, u32[]{:S(2)}) collective-permute-start(bf16[2,3,64,1024]{3,2,1,0:T(8,128)(2,1)S(1)} %fusion.25), channel_id=1, source_target_pairs={{0,8},{4,12},{8,0},{12,4},{1,9},{5,13},{9,1},{13,5},{2,10},{6,14},... | collective-permute-start | bytes 2359304 | tf_op jit(solution)/shard_map/ppermute | solution.py:31
  306.2 69.5 %collective-permute-start.35 = (bf16[256,768]{1,0:T(8,128)(2,1)}, bf16[256,768]{1,0:T(8,128)(2,1)}, u32[]{:S(2)}, u32[]{:S(2)}) collective-permute-start(bf16[256,768]{1,0:T(8,128)(2,1)} %slice.597), channel_id=1, source_target_pairs={{0,16},{16,0},{1,17},{17,1},{2,18},{18,2},{3,19},{19,3},{4,20},{20... | collective-permute-start | bytes 1179656 | tf_op jit(solution)/shard_map/ppermute | solution.py:31
  327.7 52.5 %collective-permute-start.50 = (bf16[2,2,96,768]{3,2,1,0:T(8,128)(2,1)}, bf16[2,2,96,768]{3,2,1,0:T(8,128)(2,1)}, u32[]{:S(2)}, u32[]{:S(2)}) collective-permute-start(bf16[2,2,96,768]{3,2,1,0:T(8,128)(2,1)} %broadcast_select_fusion.16), channel_id=1, source_target_pairs={{0,1},{1,0},{2,3},{3,2},{4,5},{5,4},{6,7},{7,6},{8,9},{9,8},{10,11... | collective-permute-start | bytes 1769480 | tf_op jit(solution)/shard_map/ppermute | solution.py:31
  346.9 25.9 %collective-permute-start.31 = (bf16[576,256]{1,0:T(8,128)(2,1)}, bf16[576,256]{1,0:T(8,128)(2,1)}, u32[]{:S(2)}, u32[]{:S(2)}) collective-permute-start(bf16[576,256]{1,0:T(8,128)(2,1)} %get-tuple-element.106), channel_id=1, source_target_pairs={{0,3},{1,2},{2,1},{3,0},{4,7},{5,6},{6,5},{7,4},{8,11},{9,10},{10,... | collective-permute-start | bytes 884744 | tf_op jit(solution)/shard_map/ppermute | solution.py:31
  357.5 24.2 %collective-permute-start.41 = (bf16[4,96,768]{2,1,0:T(8,128)(2,1)S(1)}, bf16[4,96,768]{2,1,0:T(8,128)(2,1)S(1)}, u32[]{:S(2)}, u32[]{:S(2)}) collective-permute-start(bf16[4,96,768]{2,1,0:T(8,128)(2,1)S(1)} %broadcast_select_fusion.19), channel_id=1, source_target_pairs={{0,4},{4,0},{8,12},{12,8},{1,5},{5,1},{9,13},{13,9},{2,6},{6,2},{1... | collective-permute-start | bytes 1769480 | tf_op jit(solution)/shard_map/ppermute | solution.py:31
  402.8 19.0 %collective-permute-start.53 = (bf16[4,48,768]{2,1,0:T(8,128)(2,1)S(1)}, bf16[4,48,768]{2,1,0:T(8,128)(2,1)S(1)}, u32[]{:S(2)}, u32[]{:S(2)}) collective-permute-start(bf16[4,48,768]{2,1,0:T(8,128)(2,1)S(1)} %pad_maximum_fusion.29), channel_id=1, source_target_pairs={{0,2},{1,3},{2,0},{3,1},{4,6},{5,7},{6,4},{7,5},{8,10},{9,11},{10,... | collective-permute-start | bytes 884744 | tf_op jit(solution)/shard_map/ppermute | solution.py:31
  407.3 22.5 %collective-permute-start.45 = (bf16[2,5,48,384]{3,2,1,0:T(8,128)(2,1)S(1)}, bf16[2,5,48,384]{3,2,1,0:T(8,128)(2,1)S(1)}, u32[]{:S(2)}, u32[]{:S(2)}) collective-permute-start(bf16[2,5,48,384]{3,2,1,0:T(8,128)(2,1)S(1)} %pad_maximum_fusion.27), channel_id=1, source_target_pairs={{0,2},{1,3},{2,0},{3,1},{4,6},{5,7},{6,4},{7,5},{8,10},{9,11},{10,... | collective-permute-start | bytes 1105928 | tf_op jit(solution)/shard_map/ppermute | solution.py:31
  421.9 23.4 %collective-permute-start.54 = (bf16[4,96,768]{2,1,0:T(8,128)(2,1)S(1)}, bf16[4,96,768]{2,1,0:T(8,128)(2,1)S(1)}, u32[]{:S(2)}, u32[]{:S(2)}) collective-permute-start(bf16[4,96,768]{2,1,0:T(8,128)(2,1)S(1)} %pad_maximum_fusion.25), channel_id=1, source_target_pairs={{0,1},{1,0},{2,3},{3,2},{4,5},{5,4},{6,7},{7,6},{8,9},{9,8},{10,11... | collective-permute-start | bytes 1769480 | tf_op jit(solution)/shard_map/ppermute | solution.py:31
  445.6 42.9 %collective-permute-start.55 = (bf16[4,192,768]{2,1,0:T(8,128)(2,1)S(1)}, bf16[4,192,768]{2,1,0:T(8,128)(2,1)S(1)}, u32[]{:S(2)}, u32[]{:S(2)}) collective-permute-start(bf16[4,192,768]{2,1,0:T(8,128)(2,1)S(1)} %pad_maximum_fusion.16), channel_id=1, source_target_pairs={{0,8},{4,12},{8,0},{12,4},{1,9},{5,13},{9,1},{13,5},{2,10},{6,14},... | collective-permute-start | bytes 3538952 | tf_op jit(solution)/shard_map/ppermute | solution.py:31
  446.6 38.8 %collective-permute-start.46 = (bf16[16,48,384]{2,1,0:T(8,128)(2,1)S(1)}, bf16[16,48,384]{2,1,0:T(8,128)(2,1)S(1)}, u32[]{:S(2)}, u32[]{:S(2)}) collective-permute-start(bf16[16,48,384]{2,1,0:T(8,128)(2,1)S(1)} %pad_maximum_fusion.24), channel_id=1, source_target_pairs={{0,8},{4,12},{8,0},{12,4},{1,9},{5,13},{9,1},{13,5},{2,10},{6,14},... | collective-permute-start | bytes 1769480 | tf_op jit(solution)/shard_map/ppermute | solution.py:31
  449.2 48.3 %collective-permute-start.22 = (bf16[192,256]{1,0:T(8,128)(2,1)S(1)}, bf16[192,256]{1,0:T(8,128)(2,1)S(1)}, u32[]{:S(2)}, u32[]{:S(2)}) collective-permute-start(bf16[192,256]{1,0:T(8,128)(2,1)S(1)} %get-tuple-element.137), channel_id=1, source_target_pairs={{0,1},{1,0},{2,3},{3,2},{4,5},{5,4},{6,7},{7,6},{8,9},{9,8},{10,11... | collective-permute-start | bytes 294920 | tf_op jit(solution)/shard_map/ppermute | solution.py:31
  451.4 43.3 %collective-permute-start.37 = (f32[9216]{0:T(1024)S(1)}, f32[9216]{0:T(1024)S(1)}, u32[]{:S(2)}, u32[]{:S(2)}) collective-permute-start(f32[9216]{0:T(1024)S(1)} %add.344), channel_id=1, source_target_pairs={{0,8},{4,12},{8,0},{12,4},{1,9},{5,13},{9,1},{13,5},{2,10},{6,14},... | collective-permute-start | bytes 110600 | tf_op jit(solution)/shard_map/ppermute | solution.py:31
  486.8 28.0 %collective-permute-start.47 = (bf16[16,96,384]{2,1,0:T(8,128)(2,1)}, bf16[16,96,384]{2,1,0:T(8,128)(2,1)}, u32[]{:S(2)}, u32[]{:S(2)}) collective-permute-start(bf16[16,96,384]{2,1,0:T(8,128)(2,1)} %pad_maximum_fusion.15), channel_id=1, source_target_pairs={{0,4},{4,0},{8,12},{12,8},{1,5},{5,1},{9,13},{13,9},{2,6},{6,2},{1... | collective-permute-start | bytes 3538952 | tf_op jit(solution)/shard_map/ppermute | solution.py:31
  491.2 35.4 %collective-permute-start.56 = (bf16[1,4,384,768]{3,2,1,0:T(8,128)(2,1)}, bf16[1,4,384,768]{3,2,1,0:T(8,128)(2,1)}, u32[]{:S(2)}, u32[]{:S(2)}) collective-permute-start(bf16[1,4,384,768]{3,2,1,0:T(8,128)(2,1)} %maximum_bitcast_fusion), channel_id=1, source_target_pairs={{0,4},{4,0},{8,12},{12,8},{1,5},{5,1},{9,13},{13,9},{2,6},{6,2},{1... | collective-permute-start | bytes 7077896 | tf_op jit(solution)/shard_map/ppermute | solution.py:31
  (101 other events, 981.6 us)
